TPU v7x, 128 devices: a whole 4x4x4 slice. The times are simulated.
128 devices in a mesh: lat: 16 (over x, y_lo, core), dep: 8 (over y_hi, z).
Axes of the slice: x: 4, y: 4 (y_hi: 2, y_lo: 2; y = y_hi * 2 + y_lo), z: 4, core: 2. Of those that a mesh axis runs over, the one named last changes fastest.
Arguments:
- crystal: float32 [2, 128, 4096, 256], P(None, 'dep', 'lat'), may hold values from -6 to 6
- beam_probe: float32 [2, 256, 256], replicated, may hold values from -1.25 to 1.25
- amplitudes: float32 [128, 256, 256], P('lat'), may hold values from 0.2 to 3
- starts: int32 [128], P('lat'), may hold values from 0 to 127
- shears: int32 [128], P('dep'), may hold values from -32 to 32
Outputs:
- updated: float32 [2, 128, 4096, 256], P(None, 'dep', 'lat')
All inputs are finite; a program needn't handle non-finite values.
Results may differ from a plain program's by a relative error of at most 0.0003.
Values sent between devices are 32-bit elements; how exact they have to be, the bound alone decides.
No kernel may reach another device: no remote copies, remote signals or barrier semaphores. Data moves between devices by JAX's collectives and lax.ppermute only.
A program may use at most 192 MiB of HBM per device.

v0:
```python
import functools
import math

import jax
import jax.numpy as jnp
import ml_dtypes
import numpy as np
from jax import lax
from jax.experimental import pallas as pl
from jax.experimental.pallas import tpu as pltpu
from jax.sharding import PartitionSpec as P

BX = 256
SH = 32
HALF = 128
QUARTER = 64
WIDE = 320
PART = 160
FULL = 384
DEP = 8

step_size = 0.5
amp_floor = 0.5
f32 = jnp.float32
bf16 = jnp.bfloat16
VMEM_LIMIT = 24 * 1024 * 1024


def vmem():
    return pl.BlockSpec(memory_space=pltpu.VMEM)


def smem():
    return pl.BlockSpec(memory_space=pltpu.SMEM)


def anywhere():
    return pl.BlockSpec(memory_space=pl.ANY)


def params():
    return pltpu.CompilerParams(vmem_limit_bytes=VMEM_LIMIT)


def kept(shape):
    return pltpu.VMEM(shape, f32)


def held(*arrays):
    return tuple(pltpu.with_memory_space_constraint(a, pltpu.VMEM) for a in arrays)


def split_np(table):
    high = table.astype(ml_dtypes.bfloat16).astype(np.float64)
    low = table - high
    return high, low


def tables(sets):
    size = BX // sets
    u = np.arange(size)
    forward, inverse = [], []
    for q in range(sets):
        angle = 2.0 * math.pi * ((u[None, :] * (sets * u[:, None] + q)) % BX) / BX
        cos, sin = np.cos(angle) / 16.0, np.sin(angle) / 16.0
        forward.append(np.block([[cos, sin], [-sin, cos]]))
        inverse.append(np.block([[cos.T, -sin.T], [sin.T, cos.T]]))
    return forward + inverse


def packed_tables():
    def beside(m, axis):
        h, l = split_np(m)
        return np.concatenate([h, h, l], axis=axis)

    lefts = np.stack([beside(m, 1) for m in tables(4)])
    rights = np.stack([beside(m.T, 0) for m in tables(2)])
    order = np.concatenate([np.arange(0, BX, 2), np.arange(1, BX, 2)])
    pick = np.zeros((BX, BX))
    pick[order, np.arange(BX)] = 1.0
    return tuple(jnp.asarray(m.astype(ml_dtypes.bfloat16)) for m in (lefts, rights, pick))


def place():
    z = lax.axis_index("dep") % 4
    return z // 2, z % 2


def partial_kernel(other, shears_in, crystal, *rest):
    first, second, buf, shears, sems, shears_sem = rest[-6:]
    shears_copy = pltpu.make_async_copy(shears_in, shears, shears_sem)
    shears_copy.start()
    half, part = place()
    half = 1 - half if other else half
    part = part if other else 1 - part
    layers = buf.shape[1]
    group = 4
    lanes = pl.ds(pl.multiple_of(half * HALF, HALF), HALF)
    copies = []
    for g in range(layers // group):
        copy = pltpu.make_async_copy(
            crystal.at[:, pl.ds(g * group, group), :, lanes],
            buf.at[:, pl.ds(g * group, group), pl.ds(2 * SH, BX), :],
            sems.at[g],
        )
        copy.start()
        copies.append(copy)
    pad = jnp.zeros((2, layers, 2 * SH, HALF), f32)
    buf[:, :, : 2 * SH, :] = pad
    buf[:, :, 2 * SH + BX :, :] = pad
    shears_copy.wait()
    for g in range(layers // group):
        copies[g].wait()
        for out, c in ((first, part), (second, 1 - part)):
            total = None if g == 0 else out[...]
            for i in range(group):
                z = g * group + i
                piece = buf[c, z, pl.ds(SH + shears[z], WIDE), :]
                total = piece if total is None else total + piece
            out[...] = total


def partial_sums(crystal, shears, other, *after):
    layers = crystal.shape[1]
    block = kept((WIDE, HALF))
    return pl.pallas_call(
        functools.partial(partial_kernel, other),
        out_shape=(block, block, kept((2, layers, BX + 4 * SH, HALF))),
        in_specs=[anywhere()] * (2 + len(after)),
        out_specs=(vmem(), vmem(), vmem()),
        scratch_shapes=[
            pltpu.SMEM(shears.shape, jnp.int32),
            pltpu.SemaphoreType.DMA((layers // 4,)),
            pltpu.SemaphoreType.DMA,
        ],
        compiler_params=params(),
    )(*(pltpu.with_memory_space_constraint(a, pltpu.HBM) for a in (shears, crystal)), *held(*after))


def sum_kernel(a, b, c, d, unused, out):
    out[...] = (a[...] + b[...]) + (c[...] + d[...])


def sum_blocks(*blocks):
    return pl.pallas_call(
        sum_kernel,
        out_shape=kept(blocks[0].shape),
        in_specs=[vmem()] * 4 + [anywhere()],
        out_specs=vmem(),
        compiler_params=params(),
    )(*held(*blocks))


def edges_kernel(own, own2, out, to_left, to_right):
    total = own[...] + own2[...]
    out[...] = total
    to_left[...] = total[:PART]
    to_right[...] = total[WIDE - SH :]


def edges(*blocks):
    return pl.pallas_call(
        edges_kernel,
        out_shape=(kept((WIDE, HALF)), kept((PART, HALF)), kept((SH, HALF))),
        in_specs=[vmem()] * 2,
        out_specs=(vmem(), vmem(), vmem()),
        compiler_params=params(),
    )(*held(*blocks))


def finish_kernel(own, left, right, out):
    out[: WIDE - SH, :] = own[SH:, :]
    out[WIDE - SH :, :] = jnp.zeros((FULL - WIDE + SH, HALF), f32)
    out[:SH, :] += left[...]
    out[FULL - PART :, :] += right[...]


def finish(*blocks):
    return pl.pallas_call(
        finish_kernel,
        out_shape=kept((FULL, HALF)),
        in_specs=[vmem()] * 3,
        out_specs=vmem(),
        compiler_params=params(),
    )(*held(*blocks))


def split3(x):
    a = x.astype(bf16)
    r = x - a.astype(f32)
    b = r.astype(bf16)
    return a, b, (r - b.astype(f32)).astype(bf16)


def prepare_kernel(amps, probe, pick, amps_out, back_out, moved):
    table = pick[...]

    def one(p, carry):
        a, b, c = split3(amps[p])
        total = (
            jnp.dot(a, table, preferred_element_type=f32)
            + jnp.dot(b, table, preferred_element_type=f32)
            + jnp.dot(c, table, preferred_element_type=f32)
        )
        for h in range(2):
            lanes = slice(h * HALF, (h + 1) * HALF)
            moved[h] = total[:, lanes]
            for q in range(4):
                amps_out[p, q * QUARTER : (q + 1) * QUARTER, lanes] = moved[h, pl.ds(q, QUARTER, stride=4), :]
        return carry

    lax.fori_loop(0, amps.shape[0], one, 0)
    re, im = probe[0], probe[1]
    peak = jnp.max(re * re + im * im)
    back_out[0] = step_size * re / peak
    back_out[1] = step_size * im / peak


def prepare(amplitudes, beam_probe, pick):
    return pl.pallas_call(
        prepare_kernel,
        out_shape=(kept(amplitudes.shape), kept(beam_probe.shape)),
        in_specs=[vmem()] * 3,
        out_specs=(vmem(), vmem()),
        scratch_shapes=[pltpu.VMEM((2, BX, HALF), f32)],
        compiler_params=params(),
    )(*held(amplitudes, beam_probe, pick))


def split2(x):
    a = x.astype(bf16)
    return a, (x - a.astype(f32)).astype(bf16)


def along_rows(table, stacked):
    high, low = split2(stacked)
    return jnp.dot(table, jnp.concatenate([high, low, high], axis=0), preferred_element_type=f32)


def along_lanes(stacked, table):
    high, low = split2(stacked)
    return jnp.dot(jnp.concatenate([high, low, high], axis=1), table, preferred_element_type=f32)


def lanes_of(turn):
    half, _ = place()
    return pl.ds(pl.multiple_of((half ^ turn) * HALF, HALF), HALF)


def fill(t, own, other):
    _, part = place()
    t[part] = own[...]
    t[1 - part] = other[...]


def both(first, second):
    return [a + b for a, b in zip(first, second)], [a - b for a, b in zip(first, second)]


def stack_rows(*parts):
    return jnp.concatenate(parts, axis=0)


def row_bins(turn, pair, starts, t, probe, lefts):
    lanes = lanes_of(turn)
    sets = [[], [], [], []]
    for p in pair:
        s = starts[p]
        re, im = t[0, pl.ds(s, BX), :], t[1, pl.ds(s, BX), :]
        pr, pi = probe[0, :, lanes], probe[1, :, lanes]
        waves = (pr * re - pi * im, pr * im + pi * re)
        s0, s1 = both([w[:QUARTER] for w in waves], [w[HALF : HALF + QUARTER] for w in waves])
        t0, t1 = both([w[QUARTER:HALF] for w in waves], [w[HALF + QUARTER :] for w in waves])
        sets[0].append(stack_rows(s0[0] + t0[0], s0[1] + t0[1]))
        sets[1].append(stack_rows(s1[0] + t1[1], s1[1] - t1[0]))
        sets[2].append(stack_rows(s0[0] - t0[0], s0[1] - t0[1]))
        sets[3].append(stack_rows(s1[0] - t1[1], s1[1] + t1[0]))
    bins = [along_rows(lefts[q], jnp.concatenate(sets[q], axis=1)) for q in range(4)]
    return [[b[:, j * HALF : (j + 1) * HALF] for b in bins] for j in range(2)]


def first_kernel(starts, own, one, probe, lefts, out, t):
    fill(t, own, one)

    def pair(i, carry):
        for j, bins in enumerate(row_bins(0, (2 * i, 2 * i + 1), starts, t, probe, lefts)):
            for q in range(4):
                out[2 * i + j, q] = bins[q]
        return carry

    lax.fori_loop(0, starts.shape[0] // 2, pair, 0, unroll=2)


def first_half(starts, own, one, beam_probe, lefts):
    return pl.pallas_call(
        first_kernel,
        out_shape=kept((starts.shape[0], 4, 2 * QUARTER, HALF)),
        in_specs=[smem()] + [vmem()] * 4,
        out_specs=vmem(),
        scratch_shapes=[pltpu.VMEM((2, FULL, HALF), f32)],
        compiler_params=params(),
    )(starts, *held(own, one, beam_probe, lefts))


def positions_kernel(starts, mine, two, three, probe, back, amps, lefts, rights, g_out, right_out, left_out, t):
    fill(t, two, three)
    g_out[...] = jnp.zeros(g_out.shape, f32)
    sides = (slice(0, HALF), slice(HALF, BX))
    count = starts.shape[0]
    bins, far_field, change = {}, {}, {}

    def lanes_forward(p):
        even, odd = [], []
        for a, b in zip([mine[p, q] for q in range(4)], bins.pop(p)):
            total, rest = a + b, a - b
            even.append(jnp.concatenate([total[:QUARTER], total[QUARTER:]], axis=1))
            odd.append(jnp.concatenate([rest[:QUARTER], rest[QUARTER:]], axis=1))
        far_field[p] = [along_lanes(stack_rows(*rows), rights[lp]) for lp, rows in ((0, even), (1, odd))]

    def project(p):
        backs = []
        for lp, f in enumerate(far_field.pop(p)):
            fr, fi = f[:, :HALF], f[:, HALF:]
            modulus2 = jnp.maximum(fr * fr + fi * fi, amp_floor * amp_floor)
            factor = amps[p, :, sides[lp]] * lax.rsqrt(modulus2) - 1.0
            backs.append(along_lanes(jnp.concatenate([fr * factor, fi * factor], axis=1), rights[2 + lp]))
        change[p] = backs[0] + backs[1], backs[0] - backs[1]

    def rows_back(p):
        s = starts[p]
        low, high = change.pop(p)
        sets = []
        for q in range(4):
            at = slice(q * QUARTER, (q + 1) * QUARTER)
            stacked = [jnp.concatenate([low[at, side], high[at, side]], axis=1) for side in sides]
            g = along_rows(lefts[4 + q], stack_rows(*stacked))
            sets.append((g[:QUARTER], g[QUARTER:]))
        s0, s1 = both(sets[0], sets[2])
        t0, t1 = both(sets[1], sets[3])
        diff_re = stack_rows(s0[0] + t0[0], s1[0] - t1[1], s0[0] - t0[0], s1[0] + t1[1])
        diff_im = stack_rows(s0[1] + t0[1], s1[1] + t1[0], s0[1] - t0[1], s1[1] - t1[0])
        for turn in range(2):
            dr, di = diff_re[:, sides[turn]], diff_im[:, sides[turn]]
            br, bi = back[0, :, lanes_of(turn)], back[1, :, lanes_of(turn)]
            g_out[0, turn, pl.ds(s, BX), :] += br * dr + bi * di
            g_out[1, turn, pl.ds(s, BX), :] += br * di - bi * dr

    for step in range(count + 3):
        if step < count and step % 2 == 0:
            pair = (step, step + 1)
            bins.update(zip(pair, row_bins(1, pair, starts, t, probe, lefts)))
        if 0 <= step - 1 < count:
            lanes_forward(step - 1)
        if 0 <= step - 2 < count:
            project(step - 2)
        if 0 <= step - 3:
            rows_back(step - 3)
    right_out[...] = g_out[:, :, BX - SH :, :]
    left_out[...] = g_out[:, :, :SH, :]


def positions(starts, mine, two, three, beam_probe, back, amps, lefts, rights):
    return pl.pallas_call(
        positions_kernel,
        out_shape=(kept((2, 2, FULL, HALF)), kept((2, 2, PART, HALF)), kept((2, 2, SH, HALF))),
        in_specs=[smem()] + [vmem()] * 8,
        out_specs=(vmem(), vmem(), vmem()),
        scratch_shapes=[pltpu.VMEM((2, FULL, HALF), f32)],
        compiler_params=params(),
    )(starts, *held(mine, two, three, beam_probe, back, amps, lefts, rights))


EARLY = 3
CHUNKS = BX // SH


def first_early(shear):
    return 3 + (shear > -SH).astype(jnp.int32) + (shear > 0).astype(jnp.int32)


def rows_at(chunk, count, before=0):
    return pl.ds(pl.multiple_of(chunk * SH, SH) + before, count * SH)


def update_layer(z, chunk, count, shear, far, own, changes, before, buf, at):
    for c in range(2):
        for turn, source in enumerate((own, far)):
            cells = source[c, z, rows_at(chunk, count, 2 * SH), :]
            moved = changes[c, turn, pl.ds(chunk * SH + before - shear, count * SH), :]
            buf[c, z, at * SH : (at + count) * SH, lanes_of(turn)] = cells + moved


def send_rows(z, chunk, count, buf, at, out, sem):
    source = buf.at[:, z, pl.ds(at * SH, count * SH), :]
    pltpu.make_async_copy(source, out.at[:, z, rows_at(chunk, count), :], sem).start()


def early_kernel(shears, far, own, g, out, buf, sem):
    def layer(z, carry):
        chunk = first_early(shears[z])
        update_layer(z, chunk, EARLY, shears[z], far, own, g, 0, buf, 0)
        send_rows(z, chunk, EARLY, buf, 0, out, sem)
        return carry

    lax.fori_loop(0, buf.shape[1], layer, 0)
    pltpu.make_async_copy(buf, out.at[:, :, : EARLY * SH, :], sem).wait()


def update_kernel(shears, far, own, g, left, right, begun, out, ext, buf, sem):
    ext[:, :, SH:, :] = g[:, :, : BX + SH, :]
    ext[:, :, :SH, :] = jnp.zeros((2, 2, SH, HALF), f32)
    ext[:, :, :PART, :] += left[...]
    ext[:, :, BX + SH :, :] += right[...]

    def layer(z, carry):
        begin = first_early(shears[z])
        pieces = (
            (0, 3),
            (jnp.where(begin == 3, 6, 3), 1),
            (jnp.where(begin == 5, 4, 7), 1),
        )
        at = 0
        for chunk, count in pieces:
            update_layer(z, chunk, count, shears[z], far, own, ext, SH, buf, at)
            send_rows(z, chunk, count, buf, at, out, sem)
            at += count
        return carry

    lax.fori_loop(0, buf.shape[1], layer, 0)
    pltpu.make_async_copy(buf, out.at[:, :, : (CHUNKS - EARLY) * SH, :], sem).wait()


def update_early(far, own, shears, g):
    layers = far.shape[1]
    return pl.pallas_call(
        early_kernel,
        out_shape=pltpu.HBM((2, layers, BX, BX), f32),
        in_specs=[smem()] + [vmem()] * 3,
        out_specs=pl.BlockSpec(memory_space=pltpu.HBM),
        scratch_shapes=[pltpu.VMEM((2, layers, EARLY * SH, BX), f32), pltpu.SemaphoreType.DMA],
        compiler_params=params(),
    )(shears, *held(far, own, g))


def update(far, own, shears, g, left, right, begun):
    layers = far.shape[1]
    return pl.pallas_call(
        update_kernel,
        out_shape=jax.ShapeDtypeStruct((2, layers, BX, BX), f32),
        in_specs=[smem()] + [vmem()] * 5 + [pl.BlockSpec(memory_space=pltpu.HBM)],
        out_specs=pl.BlockSpec(memory_space=pltpu.HBM),
        input_output_aliases={6: 0},
        scratch_shapes=[
            pltpu.VMEM((2, 2, BX + 2 * SH, HALF), f32),
            pltpu.VMEM((2, layers, (CHUNKS - EARLY) * SH, BX), f32),
            pltpu.SemaphoreType.DMA,
        ],
        compiler_params=params(),
    )(shears, *held(far, own, g, left, right), begun)


def depth_swap(value, by):
    return lax.ppermute(value, "dep", [(i, i ^ by) for i in range(DEP)])


def shifted(value, by):
    count = lax.axis_size("lat")
    return lax.ppermute(value, "lat", [(i, i + by) for i in range(count) if 0 <= i + by < count])


def body(crystal, beam_probe, amplitudes, starts, shears):
    lefts, rights, pick = packed_tables()
    send2, send3, far = partial_sums(crystal, shears, True)
    got3 = depth_swap(send3, 3)
    got2 = depth_swap(send2, 2)
    send1, mine, near_half = partial_sums(crystal, shears, False, send2)
    got1 = depth_swap(send1, 1)
    amps, back = prepare(amplitudes, beam_probe, pick)
    part = sum_blocks(mine, got1, got2, got3, back)
    whole, to_left, to_right = edges(part, depth_swap(part, 4))
    block = finish(whole, shifted(to_right, 1), shifted(to_left, -1))
    three = depth_swap(block, 3)
    two = depth_swap(block, 2)
    one = depth_swap(block, 1)
    bins = first_half(starts, block, one, beam_probe, lefts)
    g, to_right, to_left = positions(starts, bins, two, three, beam_probe, back, amps, lefts, rights)
    begun = update_early(far, near_half, shears, g)
    return update(far, near_half, shears, g, shifted(to_right, 1), shifted(to_left, -1), begun)


def solution(mesh):
    placed = (P(None, "dep", "lat", None), P(), P("lat", None, None), P("lat"), P("dep"))
    return jax.shard_map(
        body, mesh=mesh, in_specs=placed, out_specs=P(None, "dep", "lat", None), check_vma=False
    )
```

profile of v0, /device:TPU:3, one launch (start us, length us, event | category | flops | bytes accessed | tf_op | source)
XLA Modules:
  0.0 63.1 jit_solution(2318463847687807495)
XLA Ops:
  0.0 2.4 %shard_map.82 = (f32[320,128]{1,0:T(8,128)S(1)}, f32[320,128]{1,0:T(8,128)S(1)}, f32[2,16,384,128]{3,2,1,0:T(8,128)S(1)}) custom-call(s32[16]{0:T(128)} %shears.3, f32[2,16,256,256]{3,2,1,0:T(8,128)} %crystal.3), custom_call_target="tpu_custom_call" | custom-call | tf_op jit(solution)/shard_map/pallas_call | solution.py:126
  2.5 3.8 %collective-permute-start.2 = (f32[320,128]{1,0:T(8,128)S(1)}, f32[320,128]{1,0:T(8,128)S(1)}, u32[]{:S(2)}, u32[]{:S(2)}) collective-permute-start(f32[320,128]{1,0:T(8,128)S(1)} %get-tuple-element.24), channel_id=1, source_target_pairs={{0,3},{1,2},{2,1},{3,0},{4,7},{5,6},{6,5},{7,4},{8,11},{9,10},{10,... | collective-permute-start | bytes 491528 | tf_op jit(solution)/shard_map/ppermute | solution.py:463
  6.3 2.5 %shard_map.83 = (f32[320,128]{1,0:T(8,128)S(1)}, f32[320,128]{1,0:T(8,128)S(1)}, f32[2,16,384,128]{3,2,1,0:T(8,128)S(1)}) custom-call(s32[16]{0:T(128)} %shears.3, f32[2,16,256,256]{3,2,1,0:T(8,128)} %crystal.3, f32[320,128]{1,0:T(8,128)S(1)} %get-tuple-element.20.rest_0_), custom_call_target="tpu_custom_call" | custom-call | tf_op jit(solution)/shard_map/pallas_call | solution.py:126
  8.9 0.7 %collective-permute-start = (f32[320,128]{1,0:T(8,128)S(1)}, f32[320,128]{1,0:T(8,128)S(1)}, u32[]{:S(2)}, u32[]{:S(2)}) collective-permute-start(f32[320,128]{1,0:T(8,128)S(1)} %get-tuple-element.23), channel_id=1, source_target_pairs={{0,1},{1,0},{2,3},{3,2},{4,5},{5,4},{6,7},{7,6},{8,9},{9,8},{10,11... | collective-permute-start | bytes 491528 | tf_op jit(solution)/shard_map/ppermute | solution.py:463
  9.6 2.6 %shard_map.84 = (f32[8,256,256]{2,1,0:T(8,128)S(1)}, f32[2,256,256]{2,1,0:T(8,128)S(1)}) custom-call(f32[8,256,256]{2,1,0:T(8,128)S(1)} %copy-done.2, f32[2,256,256]{2,1,0:T(8,128)S(1)} %copy-done, bf16[256,256]{1,0:T(8,128)(2,1)S(1)} %copy-done.4), custom_call_target="tpu_custom_call" | custom-call | tf_op jit(solution)/shard_map/pallas_call | solution.py:220
  12.1 1.2 %collective-permute-done.2.d = f32[320,128]{1,0:T(8,128)S(1)} collective-permute-done((f32[320,128]{1,0:T(8,128)S(1)}, f32[320,128]{1,0:T(8,128)S(1)}, u32[]{:S(2)}, u32[]{:S(2)}) %collective-permute-start.2) | collective-permute-done | bytes 163872 | tf_op jit(solution)/shard_map/ppermute | solution.py:463
  13.3 0.7 %collective-permute-done.b = f32[320,128]{1,0:T(8,128)S(1)} collective-permute-done((f32[320,128]{1,0:T(8,128)S(1)}, f32[320,128]{1,0:T(8,128)S(1)}, u32[]{:S(2)}, u32[]{:S(2)}) %collective-permute-start) | collective-permute-done | bytes 163872 | tf_op jit(solution)/shard_map/ppermute | solution.py:463
  14.1 3.0 %collective-permute-start.3 = (f32[320,128]{1,0:T(8,128)S(1)}, f32[320,128]{1,0:T(8,128)S(1)}, u32[]{:S(2)}, u32[]{:S(2)}) collective-permute-start(f32[320,128]{1,0:T(8,128)S(1)} %shard_map.85.own), channel_id=1, source_target_pairs={{0,4},{1,5},{2,6},{3,7},{4,0},{5,1},{6,2},{7,3},{8,12},{9,13},{10,... | collective-permute-start | bytes 491528 | tf_op jit(solution)/shard_map/ppermute | solution.py:463
  17.0 2.8 %collective-permute-done.3.own2 = f32[320,128]{1,0:T(8,128)S(1)} collective-permute-done((f32[320,128]{1,0:T(8,128)S(1)}, f32[320,128]{1,0:T(8,128)S(1)}, u32[]{:S(2)}, u32[]{:S(2)}) %collective-permute-start.3) | collective-permute-done | bytes 163872 | tf_op jit(solution)/shard_map/ppermute | solution.py:463
  19.8 4.8 %collective-permute-start.5 = (f32[160,128]{1,0:T(8,128)S(1)}, f32[160,128]{1,0:T(8,128)S(1)}, u32[]{:S(2)}, u32[]{:S(2)}) collective-permute-start(f32[160,128]{1,0:T(8,128)S(1)} %get-tuple-element.28), channel_id=1, source_target_pairs={{8,0},{16,8},{24,16},{32,24},{40,32},{48,40},{56,48},{64,56},{72,6... | collective-permute-start | bytes 245768 | tf_op jit(solution)/shard_map/ppermute | solution.py:468
  24.6 3.1 %collective-permute-start.4 = (f32[32,128]{1,0:T(8,128)S(1)}, f32[32,128]{1,0:T(8,128)S(1)}, u32[]{:S(2)}, u32[]{:S(2)}) collective-permute-start(f32[32,128]{1,0:T(8,128)S(1)} %get-tuple-element.27), channel_id=1, source_target_pairs={{0,8},{8,16},{16,24},{24,32},{32,40},{40,48},{48,56},{56,64},{64,7... | collective-permute-start | bytes 49160 | tf_op jit(solution)/shard_map/ppermute | solution.py:468
  27.7 0.8 %collective-permute-done.4.left = f32[32,128]{1,0:T(8,128)S(1)} collective-permute-done((f32[32,128]{1,0:T(8,128)S(1)}, f32[32,128]{1,0:T(8,128)S(1)}, u32[]{:S(2)}, u32[]{:S(2)}) %collective-permute-start.4) | collective-permute-done | bytes 16416 | tf_op jit(solution)/shard_map/ppermute | solution.py:468
  28.6 0.9 %collective-permute-start.6 = (f32[384,128]{1,0:T(8,128)S(1)}, f32[384,128]{1,0:T(8,128)S(1)}, u32[]{:S(2)}, u32[]{:S(2)}) collective-permute-start(f32[384,128]{1,0:T(8,128)S(1)} %shard_map.87.own), channel_id=1, source_target_pairs={{0,1},{1,0},{2,3},{3,2},{4,5},{5,4},{6,7},{7,6},{8,9},{9,8},{10,11... | collective-permute-start | bytes 589832 | tf_op jit(solution)/shard_map/ppermute | solution.py:463
  29.5 2.2 %collective-permute-start.8 = (f32[384,128]{1,0:T(8,128)S(1)}, f32[384,128]{1,0:T(8,128)S(1)}, u32[]{:S(2)}, u32[]{:S(2)}) collective-permute-start(f32[384,128]{1,0:T(8,128)S(1)} %shard_map.87.own), channel_id=1, source_target_pairs={{0,3},{1,2},{2,1},{3,0},{4,7},{5,6},{6,5},{7,4},{8,11},{9,10},{10,... | collective-permute-start | bytes 589832 | tf_op jit(solution)/shard_map/ppermute | solution.py:463
  31.7 0.8 %collective-permute-start.7 = (f32[384,128]{1,0:T(8,128)S(1)}, f32[384,128]{1,0:T(8,128)S(1)}, u32[]{:S(2)}, u32[]{:S(2)}) collective-permute-start(f32[384,128]{1,0:T(8,128)S(1)} %shard_map.87.own), channel_id=1, source_target_pairs={{0,2},{1,3},{2,0},{3,1},{4,6},{5,7},{6,4},{7,5},{8,10},{9,11},{10,... | collective-permute-start | bytes 589832 | tf_op jit(solution)/shard_map/ppermute | solution.py:463
  32.5 0.7 %collective-permute-done.6.one = f32[384,128]{1,0:T(8,128)S(1)} collective-permute-done((f32[384,128]{1,0:T(8,128)S(1)}, f32[384,128]{1,0:T(8,128)S(1)}, u32[]{:S(2)}, u32[]{:S(2)}) %collective-permute-start.6) | collective-permute-done | bytes 196640 | tf_op jit(solution)/shard_map/ppermute | solution.py:463
  33.2 2.0 %shard_map.88.mine = f32[8,4,128,128]{3,2,1,0:T(8,128)S(1)} custom-call(s32[8]{0:T(128)S(1)} %copy-done.6, f32[384,128]{1,0:T(8,128)S(1)} %shard_map.87.own, f32[384,128]{1,0:T(8,128)S(1)} %collective-permute-done.6.one, f32[2,256,256]{2,1,0:T(8,128)S(1)} %copy-done, bf16[8,128,384]{2,1,0:T(8,128)(2,1)S(1)} %copy-done.1), custom_call_target="tpu_custom_call" | custom-call | tf_op jit(solution)/shard_map/pallas_call | solution.py:295
  35.8 3.8 %collective-permute-done.7.two = f32[384,128]{1,0:T(8,128)S(1)} collective-permute-done((f32[384,128]{1,0:T(8,128)S(1)}, f32[384,128]{1,0:T(8,128)S(1)}, u32[]{:S(2)}, u32[]{:S(2)}) %collective-permute-start.7) | collective-permute-done | bytes 196640 | tf_op jit(solution)/shard_map/ppermute | solution.py:463
  39.6 8.3 %shard_map.89 = (f32[2,2,384,128]{3,2,1,0:T(8,128)S(1)}, f32[2,2,160,128]{3,2,1,0:T(8,128)S(1)}, f32[2,2,32,128]{3,2,1,0:T(8,128)S(1)}) custom-call(s32[8]{0:T(128)S(1)} %copy-done.6, f32[8,4,128,128]{3,2,1,0:T(8,128)S(1)} %shard_map.88.mine, f32[384,128]{1,0:T(8,128)S(1)} %collective-permute-done.7.two, f32[384,128]{1,0:T(8,128)S(1)} %collective-permute-done.8.three, ...), custom_call_target="tpu_custom_call" | custom-call | tf_op jit(solution)/shard_map/pallas_call | solution.py:363
  47.8 5.9 %collective-permute-start.9 = (f32[2,2,160,128]{3,2,1,0:T(8,128)S(1)}, f32[2,2,160,128]{3,2,1,0:T(8,128)S(1)}, u32[]{:S(2)}, u32[]{:S(2)}) collective-permute-start(f32[2,2,160,128]{3,2,1,0:T(8,128)S(1)} %get-tuple-element.31), channel_id=1, source_target_pairs={{0,8},{8,16},{16,24},{24,32},{32,40},{40,48},{48,56},{56,64},{64,7... | collective-permute-start | bytes 983048 | tf_op jit(solution)/shard_map/ppermute | solution.py:468
  53.7 1.9 %collective-permute-start.10 = (f32[2,2,32,128]{3,2,1,0:T(8,128)S(1)}, f32[2,2,32,128]{3,2,1,0:T(8,128)S(1)}, u32[]{:S(2)}, u32[]{:S(2)}) collective-permute-start(f32[2,2,32,128]{3,2,1,0:T(8,128)S(1)} %get-tuple-element.32), channel_id=1, source_target_pairs={{8,0},{16,8},{24,16},{32,24},{40,32},{48,40},{56,48},{64,56},{72,6... | collective-permute-start | bytes 196616 | tf_op jit(solution)/shard_map/ppermute | solution.py:468
  55.6 2.2 %shard_map.90.begun = f32[2,16,256,256]{3,2,1,0:T(8,128)} custom-call(s32[16]{0:T(128)S(1)} %copy-done.5, f32[2,16,384,128]{3,2,1,0:T(8,128)S(1)} %get-tuple-element.19.far, f32[2,16,384,128]{3,2,1,0:T(8,128)S(1)} %get-tuple-element.21.own, f32[2,2,384,128]{3,2,1,0:T(8,128)S(1)} %get-tuple-element.30.g), custom_call_target="tpu_custom_call" | custom-call | tf_op jit(solution)/shard_map/pallas_call | solution.py:435
  57.9 2.3 %collective-permute-done.10.right = f32[2,2,32,128]{3,2,1,0:T(8,128)S(1)} collective-permute-done((f32[2,2,32,128]{3,2,1,0:T(8,128)S(1)}, f32[2,2,32,128]{3,2,1,0:T(8,128)S(1)}, u32[]{:S(2)}, u32[]{:S(2)}) %collective-permute-start.10) | collective-permute-done | bytes 65568 | tf_op jit(solution)/shard_map/ppermute | solution.py:468
  60.2 2.9 %shard_map.91 = f32[2,16,256,256]{3,2,1,0:T(8,128)} custom-call(s32[16]{0:T(128)S(1)} %copy-done.5, f32[2,16,384,128]{3,2,1,0:T(8,128)S(1)} %get-tuple-element.19.far, f32[2,16,384,128]{3,2,1,0:T(8,128)S(1)} %get-tuple-element.21.own, f32[2,2,384,128]{3,2,1,0:T(8,128)S(1)} %get-tuple-element.30.g, ...), custom_call_target="tpu_custom_call", output_to_operand_aliasing={{}: (6, {})} | custom-call | tf_op jit(solution)/shard_map/pallas_call | solution.py:447
  (22 shorter events, 0.7 us)
Async XLA Ops:
  2.4 7.1 %copy-start = (f32[2,256,256]{2,1,0:T(8,128)S(1)}, f32[2,256,256]{2,1,0:T(8,128)}, u32[]{:S(2)}) copy-start(f32[2,256,256]{2,1,0:T(8,128)} %probe.5) | copy-start | bytes 1572868
  2.5 7.1 %copy-start.2 = (f32[8,256,256]{2,1,0:T(8,128)S(1)}, f32[8,256,256]{2,1,0:T(8,128)}, u32[]{:S(2)}) copy-start(f32[8,256,256]{2,1,0:T(8,128)} %amps.1) | copy-start | bytes 6291460
  2.5 7.1 %copy-start.4 = (bf16[256,256]{1,0:T(8,128)(2,1)S(1)}, bf16[256,256]{1,0:T(8,128)(2,1)}, u32[]{:S(2)}) copy-start(bf16[256,256]{1,0:T(8,128)(2,1)} %constant.8.clone.pick) | copy-start | bytes 393220
  2.5 10.8 %collective-permute-start.2 = (f32[320,128]{1,0:T(8,128)S(1)}, f32[320,128]{1,0:T(8,128)S(1)}, u32[]{:S(2)}, u32[]{:S(2)}) collective-permute-start(f32[320,128]{1,0:T(8,128)S(1)} %get-tuple-element.24), channel_id=1, source_target_pairs={{0,3},{1,2},{2,1},{3,0},{4,7},{5,6},{6,5},{7,4},{8,11},{9,10},{10,... | collective-permute-start | bytes 491528 | tf_op jit(solution)/shard_map/ppermute | solution.py:463
  6.3 26.9 %copy-start.1 = (bf16[8,128,384]{2,1,0:T(8,128)(2,1)S(1)}, bf16[8,128,384]{2,1,0:T(8,128)(2,1)}, u32[]{:S(2)}) copy-start(bf16[8,128,384]{2,1,0:T(8,128)(2,1)} %constant.6.clone.lefts) | copy-start | bytes 2359300
  6.3 26.9 %copy-start.6 = (s32[8]{0:T(128)S(1)}, s32[8]{0:T(128)}, u32[]{:S(2)}) copy-start(s32[8]{0:T(128)} %starts.3) | copy-start | bytes 100
  6.3 7.0 %collective-permute-start.1 = (f32[320,128]{1,0:T(8,128)S(1)}, f32[320,128]{1,0:T(8,128)S(1)}, u32[]{:S(2)}, u32[]{:S(2)}) collective-permute-start(f32[320,128]{1,0:T(8,128)S(1)} %get-tuple-element.20.rest_0_), channel_id=1, source_target_pairs={{0,2},{1,3},{2,0},{3,1},{4,6},{5,7},{6,4},{7,5},{8,10},{9,11},{10,... | collective-permute-start | bytes 491528 | tf_op jit(solution)/shard_map/ppermute | solution.py:463
  8.9 30.7 %copy-start.3 = (bf16[4,768,256]{2,1,0:T(8,128)(2,1)S(1)}, bf16[4,768,256]{2,1,0:T(8,128)(2,1)}, u32[]{:S(2)}) copy-start(bf16[4,768,256]{2,1,0:T(8,128)(2,1)} %constant.7.clone.rights) | copy-start | bytes 4718596
  8.9 5.1 %collective-permute-start = (f32[320,128]{1,0:T(8,128)S(1)}, f32[320,128]{1,0:T(8,128)S(1)}, u32[]{:S(2)}, u32[]{:S(2)}) collective-permute-start(f32[320,128]{1,0:T(8,128)S(1)} %get-tuple-element.23), channel_id=1, source_target_pairs={{0,1},{1,0},{2,3},{3,2},{4,5},{5,4},{6,7},{7,6},{8,9},{9,8},{10,11... | collective-permute-start | bytes 491528 | tf_op jit(solution)/shard_map/ppermute | solution.py:463
  14.0 41.6 %copy-start.5 = (s32[16]{0:T(128)S(1)}, s32[16]{0:T(128)}, u32[]{:S(2)}) copy-start(s32[16]{0:T(128)} %shears.3) | copy-start | bytes 196
  14.1 5.8 %collective-permute-start.3 = (f32[320,128]{1,0:T(8,128)S(1)}, f32[320,128]{1,0:T(8,128)S(1)}, u32[]{:S(2)}, u32[]{:S(2)}) collective-permute-start(f32[320,128]{1,0:T(8,128)S(1)} %shard_map.85.own), channel_id=1, source_target_pairs={{0,4},{1,5},{2,6},{3,7},{4,0},{5,1},{6,2},{7,3},{8,12},{9,13},{10,... | collective-permute-start | bytes 491528 | tf_op jit(solution)/shard_map/ppermute | solution.py:463
  19.8 8.7 %collective-permute-start.5 = (f32[160,128]{1,0:T(8,128)S(1)}, f32[160,128]{1,0:T(8,128)S(1)}, u32[]{:S(2)}, u32[]{:S(2)}) collective-permute-start(f32[160,128]{1,0:T(8,128)S(1)} %get-tuple-element.28), channel_id=1, source_target_pairs={{8,0},{16,8},{24,16},{32,24},{40,32},{48,40},{56,48},{64,56},{72,6... | collective-permute-start | bytes 245768 | tf_op jit(solution)/shard_map/ppermute | solution.py:468
  24.6 4.0 %collective-permute-start.4 = (f32[32,128]{1,0:T(8,128)S(1)}, f32[32,128]{1,0:T(8,128)S(1)}, u32[]{:S(2)}, u32[]{:S(2)}) collective-permute-start(f32[32,128]{1,0:T(8,128)S(1)} %get-tuple-element.27), channel_id=1, source_target_pairs={{0,8},{8,16},{16,24},{24,32},{32,40},{40,48},{48,56},{56,64},{64,7... | collective-permute-start | bytes 49160 | tf_op jit(solution)/shard_map/ppermute | solution.py:468
  28.6 4.6 %collective-permute-start.6 = (f32[384,128]{1,0:T(8,128)S(1)}, f32[384,128]{1,0:T(8,128)S(1)}, u32[]{:S(2)}, u32[]{:S(2)}) collective-permute-start(f32[384,128]{1,0:T(8,128)S(1)} %shard_map.87.own), channel_id=1, source_target_pairs={{0,1},{1,0},{2,3},{3,2},{4,5},{5,4},{6,7},{7,6},{8,9},{9,8},{10,11... | collective-permute-start | bytes 589832 | tf_op jit(solution)/shard_map/ppermute | solution.py:463
  29.5 6.3 %collective-permute-start.8 = (f32[384,128]{1,0:T(8,128)S(1)}, f32[384,128]{1,0:T(8,128)S(1)}, u32[]{:S(2)}, u32[]{:S(2)}) collective-permute-start(f32[384,128]{1,0:T(8,128)S(1)} %shard_map.87.own), channel_id=1, source_target_pairs={{0,3},{1,2},{2,1},{3,0},{4,7},{5,6},{6,5},{7,4},{8,11},{9,10},{10,... | collective-permute-start | bytes 589832 | tf_op jit(solution)/shard_map/ppermute | solution.py:463
  31.7 7.9 %collective-permute-start.7 = (f32[384,128]{1,0:T(8,128)S(1)}, f32[384,128]{1,0:T(8,128)S(1)}, u32[]{:S(2)}, u32[]{:S(2)}) collective-permute-start(f32[384,128]{1,0:T(8,128)S(1)} %shard_map.87.own), channel_id=1, source_target_pairs={{0,2},{1,3},{2,0},{3,1},{4,6},{5,7},{6,4},{7,5},{8,10},{9,11},{10,... | collective-permute-start | bytes 589832 | tf_op jit(solution)/shard_map/ppermute | solution.py:463
  47.8 12.3 %collective-permute-start.9 = (f32[2,2,160,128]{3,2,1,0:T(8,128)S(1)}, f32[2,2,160,128]{3,2,1,0:T(8,128)S(1)}, u32[]{:S(2)}, u32[]{:S(2)}) collective-permute-start(f32[2,2,160,128]{3,2,1,0:T(8,128)S(1)} %get-tuple-element.31), channel_id=1, source_target_pairs={{0,8},{8,16},{16,24},{24,32},{32,40},{40,48},{48,56},{56,64},{64,7... | collective-permute-start | bytes 983048 | tf_op jit(solution)/shard_map/ppermute | solution.py:468
  53.7 6.4 %collective-permute-start.10 = (f32[2,2,32,128]{3,2,1,0:T(8,128)S(1)}, f32[2,2,32,128]{3,2,1,0:T(8,128)S(1)}, u32[]{:S(2)}, u32[]{:S(2)}) collective-permute-start(f32[2,2,32,128]{3,2,1,0:T(8,128)S(1)} %get-tuple-element.32), channel_id=1, source_target_pairs={{8,0},{16,8},{24,16},{32,24},{40,32},{48,40},{56,48},{64,56},{72,6... | collective-permute-start | bytes 196616 | tf_op jit(solution)/shard_map/ppermute | solution.py:468
where the time goes:
time: 63.4 us; the launch traced here: 63.1 us
  starting transfers between devices  27 us (43%)
  Pallas kernels  23 us (36%)
  waiting for transfers between devices  12.8 us (20%)
    ppermute x4, starting transfers between devices, shifted(): lax.ppermute(value, 'lat', [(i, i + by) for i in range(count) if 0 <= i +...  15.7 us
    ppermute x7, starting transfers between devices, depth_swap(): return lax.ppermute(value, 'dep', [(i, i ^ by) for i in range(DEP)])  11.4 us
    ppermute x7, waiting for transfers between devices, depth_swap(): return lax.ppermute(value, 'dep', [(i, i ^ by) for i in range(DEP)])  9.71 us
    pallas_call x1, Pallas kernels, positions(): pl.pallas_call(positions_kernel, out_shape=(kept((2, 2, FULL, HALF)), kep...  8.26 us
    pallas_call x2, Pallas kernels, partial_sums(): pl.pallas_call(functools.partial(partial_kernel, other), out_shape=(block...  4.97 us
    ppermute x4, waiting for transfers between devices, shifted(): lax.ppermute(value, 'lat', [(i, i + by) for i in range(count) if 0 <= i +...  3.1 us
    pallas_call x1, Pallas kernels, update(): pl.pallas_call(update_kernel, out_shape=jax.ShapeDtypeStruct((2, layers,...  2.94 us
    pallas_call x1, Pallas kernels, prepare(): pl.pallas_call(prepare_kernel, out_shape=(kept(amplitudes.shape), kept(be...  2.58 us
  transfers between devices with their start and end apart: 11, of which 8 were waited for; matrix products, arithmetic and copies ran while one was open for 0% of the time, Pallas kernels for 15%

commit v1 on v0

--- a/solution.py
+++ b/solution.py
@@ -94,7 +94,7 @@
     half = 1 - half if other else half
     part = part if other else 1 - part
     layers = buf.shape[1]
-    group = 4
+    group = 2
     lanes = pl.ds(pl.multiple_of(half * HALF, HALF), HALF)
     copies = []
     for g in range(layers // group):
@@ -130,7 +130,7 @@
         out_specs=(vmem(), vmem(), vmem()),
         scratch_shapes=[
             pltpu.SMEM(shears.shape, jnp.int32),
-            pltpu.SemaphoreType.DMA((layers // 4,)),
+            pltpu.SemaphoreType.DMA((layers // 2,)),
             pltpu.SemaphoreType.DMA,
         ],
         compiler_params=params(),
@@ -402,7 +402,7 @@
         send_rows(z, chunk, EARLY, buf, 0, out, sem)
         return carry
 
-    lax.fori_loop(0, buf.shape[1], layer, 0)
+    lax.fori_loop(0, buf.shape[1], layer, 0, unroll=2)
     pltpu.make_async_copy(buf, out.at[:, :, : EARLY * SH, :], sem).wait()
 
 
@@ -426,7 +426,7 @@
             at += count
         return carry
 
-    lax.fori_loop(0, buf.shape[1], layer, 0)
+    lax.fori_loop(0, buf.shape[1], layer, 0, unroll=2)
     pltpu.make_async_copy(buf, out.at[:, :, : (CHUNKS - EARLY) * SH, :], sem).wait()
 
 

time: 63.4 us -> 63.2 us (level)
  no operation moved by 1% of the time
where the time goes in v1:
time: 63.2 us; the launch traced here: 62.9 us
  starting transfers between devices  27 us (43%)
  Pallas kernels  22.8 us (36%)
  waiting for transfers between devices  12.9 us (20%)
    ppermute x4, starting transfers between devices, shifted(): lax.ppermute(value, 'lat', [(i, i + by) for i in range(count) if 0 <= i +...  15.7 us
    ppermute x7, starting transfers between devices, depth_swap(): return lax.ppermute(value, 'dep', [(i, i ^ by) for i in range(DEP)])  11.3 us
    ppermute x7, waiting for transfers between devices, depth_swap(): return lax.ppermute(value, 'dep', [(i, i ^ by) for i in range(DEP)])  9.81 us
    pallas_call x1, Pallas kernels, positions(): pl.pallas_call(positions_kernel, out_shape=(kept((2, 2, FULL, HALF)), kep...  8.18 us
    pallas_call x2, Pallas kernels, partial_sums(): pl.pallas_call(functools.partial(partial_kernel, other), out_shape=(block...  4.82 us
    ppermute x4, waiting for transfers between devices, shifted(): lax.ppermute(value, 'lat', [(i, i + by) for i in range(count) if 0 <= i +...  3.12 us
    pallas_call x1, Pallas kernels, update(): pl.pallas_call(update_kernel, out_shape=jax.ShapeDtypeStruct((2, layers,...  2.92 us
    pallas_call x1, Pallas kernels, prepare(): pl.pallas_call(prepare_kernel, out_shape=(kept(amplitudes.shape), kept(be...  2.58 us
  transfers between devices with their start and end apart: 11, of which 8 were waited for; matrix products, arithmetic and copies ran while one was open for 0% of the time, Pallas kernels for 15%

profile of v1, /device:TPU:3, one launch (start us, length us, event | category | flops | bytes accessed | tf_op | source)
XLA Modules:
  0.0 62.9 jit_solution(8477132931818263534)
XLA Ops:
  0.0 2.4 %shard_map.82 = (f32[320,128]{1,0:T(8,128)S(1)}, f32[320,128]{1,0:T(8,128)S(1)}, f32[2,16,384,128]{3,2,1,0:T(8,128)S(1)}) custom-call(s32[16]{0:T(128)} %shears.3, f32[2,16,256,256]{3,2,1,0:T(8,128)} %crystal.3), custom_call_target="tpu_custom_call" | custom-call | tf_op jit(solution)/shard_map/pallas_call | solution.py:126
  2.4 3.8 %collective-permute-start.2 = (f32[320,128]{1,0:T(8,128)S(1)}, f32[320,128]{1,0:T(8,128)S(1)}, u32[]{:S(2)}, u32[]{:S(2)}) collective-permute-start(f32[320,128]{1,0:T(8,128)S(1)} %get-tuple-element.24), channel_id=1, source_target_pairs={{0,3},{1,2},{2,1},{3,0},{4,7},{5,6},{6,5},{7,4},{8,11},{9,10},{10,... | collective-permute-start | bytes 491528 | tf_op jit(solution)/shard_map/ppermute | solution.py:463
  6.3 2.5 %shard_map.83 = (f32[320,128]{1,0:T(8,128)S(1)}, f32[320,128]{1,0:T(8,128)S(1)}, f32[2,16,384,128]{3,2,1,0:T(8,128)S(1)}) custom-call(s32[16]{0:T(128)} %shears.3, f32[2,16,256,256]{3,2,1,0:T(8,128)} %crystal.3, f32[320,128]{1,0:T(8,128)S(1)} %get-tuple-element.20.rest_0_), custom_call_target="tpu_custom_call" | custom-call | tf_op jit(solution)/shard_map/pallas_call | solution.py:126
  8.7 0.7 %collective-permute-start = (f32[320,128]{1,0:T(8,128)S(1)}, f32[320,128]{1,0:T(8,128)S(1)}, u32[]{:S(2)}, u32[]{:S(2)}) collective-permute-start(f32[320,128]{1,0:T(8,128)S(1)} %get-tuple-element.23), channel_id=1, source_target_pairs={{0,1},{1,0},{2,3},{3,2},{4,5},{5,4},{6,7},{7,6},{8,9},{9,8},{10,11... | collective-permute-start | bytes 491528 | tf_op jit(solution)/shard_map/ppermute | solution.py:463
  9.4 2.6 %shard_map.84 = (f32[8,256,256]{2,1,0:T(8,128)S(1)}, f32[2,256,256]{2,1,0:T(8,128)S(1)}) custom-call(f32[8,256,256]{2,1,0:T(8,128)S(1)} %copy-done.2, f32[2,256,256]{2,1,0:T(8,128)S(1)} %copy-done, bf16[256,256]{1,0:T(8,128)(2,1)S(1)} %copy-done.4), custom_call_target="tpu_custom_call" | custom-call | tf_op jit(solution)/shard_map/pallas_call | solution.py:220
  12.0 1.2 %collective-permute-done.2.d = f32[320,128]{1,0:T(8,128)S(1)} collective-permute-done((f32[320,128]{1,0:T(8,128)S(1)}, f32[320,128]{1,0:T(8,128)S(1)}, u32[]{:S(2)}, u32[]{:S(2)}) %collective-permute-start.2) | collective-permute-done | bytes 163872 | tf_op jit(solution)/shard_map/ppermute | solution.py:463
  13.2 0.8 %collective-permute-done.b = f32[320,128]{1,0:T(8,128)S(1)} collective-permute-done((f32[320,128]{1,0:T(8,128)S(1)}, f32[320,128]{1,0:T(8,128)S(1)}, u32[]{:S(2)}, u32[]{:S(2)}) %collective-permute-start) | collective-permute-done | bytes 163872 | tf_op jit(solution)/shard_map/ppermute | solution.py:463
  14.1 3.0 %collective-permute-start.3 = (f32[320,128]{1,0:T(8,128)S(1)}, f32[320,128]{1,0:T(8,128)S(1)}, u32[]{:S(2)}, u32[]{:S(2)}) collective-permute-start(f32[320,128]{1,0:T(8,128)S(1)} %shard_map.85.own), channel_id=1, source_target_pairs={{0,4},{1,5},{2,6},{3,7},{4,0},{5,1},{6,2},{7,3},{8,12},{9,13},{10,... | collective-permute-start | bytes 491528 | tf_op jit(solution)/shard_map/ppermute | solution.py:463
  17.1 2.8 %collective-permute-done.3.own2 = f32[320,128]{1,0:T(8,128)S(1)} collective-permute-done((f32[320,128]{1,0:T(8,128)S(1)}, f32[320,128]{1,0:T(8,128)S(1)}, u32[]{:S(2)}, u32[]{:S(2)}) %collective-permute-start.3) | collective-permute-done | bytes 163872 | tf_op jit(solution)/shard_map/ppermute | solution.py:463
  19.8 4.7 %collective-permute-start.5 = (f32[160,128]{1,0:T(8,128)S(1)}, f32[160,128]{1,0:T(8,128)S(1)}, u32[]{:S(2)}, u32[]{:S(2)}) collective-permute-start(f32[160,128]{1,0:T(8,128)S(1)} %get-tuple-element.28), channel_id=1, source_target_pairs={{8,0},{16,8},{24,16},{32,24},{40,32},{48,40},{56,48},{64,56},{72,6... | collective-permute-start | bytes 245768 | tf_op jit(solution)/shard_map/ppermute | solution.py:468
  24.5 3.1 %collective-permute-start.4 = (f32[32,128]{1,0:T(8,128)S(1)}, f32[32,128]{1,0:T(8,128)S(1)}, u32[]{:S(2)}, u32[]{:S(2)}) collective-permute-start(f32[32,128]{1,0:T(8,128)S(1)} %get-tuple-element.27), channel_id=1, source_target_pairs={{0,8},{8,16},{16,24},{24,32},{32,40},{40,48},{48,56},{56,64},{64,7... | collective-permute-start | bytes 49160 | tf_op jit(solution)/shard_map/ppermute | solution.py:468
  27.7 0.8 %collective-permute-done.4.left = f32[32,128]{1,0:T(8,128)S(1)} collective-permute-done((f32[32,128]{1,0:T(8,128)S(1)}, f32[32,128]{1,0:T(8,128)S(1)}, u32[]{:S(2)}, u32[]{:S(2)}) %collective-permute-start.4) | collective-permute-done | bytes 16416 | tf_op jit(solution)/shard_map/ppermute | solution.py:468
  28.5 0.9 %collective-permute-start.6 = (f32[384,128]{1,0:T(8,128)S(1)}, f32[384,128]{1,0:T(8,128)S(1)}, u32[]{:S(2)}, u32[]{:S(2)}) collective-permute-start(f32[384,128]{1,0:T(8,128)S(1)} %shard_map.87.own), channel_id=1, source_target_pairs={{0,1},{1,0},{2,3},{3,2},{4,5},{5,4},{6,7},{7,6},{8,9},{9,8},{10,11... | collective-permute-start | bytes 589832 | tf_op jit(solution)/shard_map/ppermute | solution.py:463
  29.4 2.2 %collective-permute-start.8 = (f32[384,128]{1,0:T(8,128)S(1)}, f32[384,128]{1,0:T(8,128)S(1)}, u32[]{:S(2)}, u32[]{:S(2)}) collective-permute-start(f32[384,128]{1,0:T(8,128)S(1)} %shard_map.87.own), channel_id=1, source_target_pairs={{0,3},{1,2},{2,1},{3,0},{4,7},{5,6},{6,5},{7,4},{8,11},{9,10},{10,... | collective-permute-start | bytes 589832 | tf_op jit(solution)/shard_map/ppermute | solution.py:463
  31.6 0.8 %collective-permute-start.7 = (f32[384,128]{1,0:T(8,128)S(1)}, f32[384,128]{1,0:T(8,128)S(1)}, u32[]{:S(2)}, u32[]{:S(2)}) collective-permute-start(f32[384,128]{1,0:T(8,128)S(1)} %shard_map.87.own), channel_id=1, source_target_pairs={{0,2},{1,3},{2,0},{3,1},{4,6},{5,7},{6,4},{7,5},{8,10},{9,11},{10,... | collective-permute-start | bytes 589832 | tf_op jit(solution)/shard_map/ppermute | solution.py:463
  32.4 0.8 %collective-permute-done.6.one = f32[384,128]{1,0:T(8,128)S(1)} collective-permute-done((f32[384,128]{1,0:T(8,128)S(1)}, f32[384,128]{1,0:T(8,128)S(1)}, u32[]{:S(2)}, u32[]{:S(2)}) %collective-permute-start.6) | collective-permute-done | bytes 196640 | tf_op jit(solution)/shard_map/ppermute | solution.py:463
  33.1 2.0 %shard_map.88.mine = f32[8,4,128,128]{3,2,1,0:T(8,128)S(1)} custom-call(s32[8]{0:T(128)S(1)} %copy-done.6, f32[384,128]{1,0:T(8,128)S(1)} %shard_map.87.own, f32[384,128]{1,0:T(8,128)S(1)} %collective-permute-done.6.one, f32[2,256,256]{2,1,0:T(8,128)S(1)} %copy-done, bf16[8,128,384]{2,1,0:T(8,128)(2,1)S(1)} %copy-done.1), custom_call_target="tpu_custom_call" | custom-call | tf_op jit(solution)/shard_map/pallas_call | solution.py:295
  35.5 3.9 %collective-permute-done.7.two = f32[384,128]{1,0:T(8,128)S(1)} collective-permute-done((f32[384,128]{1,0:T(8,128)S(1)}, f32[384,128]{1,0:T(8,128)S(1)}, u32[]{:S(2)}, u32[]{:S(2)}) %collective-permute-start.7) | collective-permute-done | bytes 196640 | tf_op jit(solution)/shard_map/ppermute | solution.py:463
  39.4 8.2 %shard_map.89 = (f32[2,2,384,128]{3,2,1,0:T(8,128)S(1)}, f32[2,2,160,128]{3,2,1,0:T(8,128)S(1)}, f32[2,2,32,128]{3,2,1,0:T(8,128)S(1)}) custom-call(s32[8]{0:T(128)S(1)} %copy-done.6, f32[8,4,128,128]{3,2,1,0:T(8,128)S(1)} %shard_map.88.mine, f32[384,128]{1,0:T(8,128)S(1)} %collective-permute-done.7.two, f32[384,128]{1,0:T(8,128)S(1)} %collective-permute-done.8.three, ...), custom_call_target="tpu_custom_call" | custom-call | tf_op jit(solution)/shard_map/pallas_call | solution.py:363
  47.6 6.0 %collective-permute-start.9 = (f32[2,2,160,128]{3,2,1,0:T(8,128)S(1)}, f32[2,2,160,128]{3,2,1,0:T(8,128)S(1)}, u32[]{:S(2)}, u32[]{:S(2)}) collective-permute-start(f32[2,2,160,128]{3,2,1,0:T(8,128)S(1)} %get-tuple-element.31), channel_id=1, source_target_pairs={{0,8},{8,16},{16,24},{24,32},{32,40},{40,48},{48,56},{56,64},{64,7... | collective-permute-start | bytes 983048 | tf_op jit(solution)/shard_map/ppermute | solution.py:468
  53.5 1.9 %collective-permute-start.10 = (f32[2,2,32,128]{3,2,1,0:T(8,128)S(1)}, f32[2,2,32,128]{3,2,1,0:T(8,128)S(1)}, u32[]{:S(2)}, u32[]{:S(2)}) collective-permute-start(f32[2,2,32,128]{3,2,1,0:T(8,128)S(1)} %get-tuple-element.32), channel_id=1, source_target_pairs={{8,0},{16,8},{24,16},{32,24},{40,32},{48,40},{56,48},{64,56},{72,6... | collective-permute-start | bytes 196616 | tf_op jit(solution)/shard_map/ppermute | solution.py:468
  55.5 2.2 %shard_map.90.begun = f32[2,16,256,256]{3,2,1,0:T(8,128)} custom-call(s32[16]{0:T(128)S(1)} %copy-done.5, f32[2,16,384,128]{3,2,1,0:T(8,128)S(1)} %get-tuple-element.19.far, f32[2,16,384,128]{3,2,1,0:T(8,128)S(1)} %get-tuple-element.21.own, f32[2,2,384,128]{3,2,1,0:T(8,128)S(1)} %get-tuple-element.30.g), custom_call_target="tpu_custom_call" | custom-call | tf_op jit(solution)/shard_map/pallas_call | solution.py:435
  57.7 2.3 %collective-permute-done.10.right = f32[2,2,32,128]{3,2,1,0:T(8,128)S(1)} collective-permute-done((f32[2,2,32,128]{3,2,1,0:T(8,128)S(1)}, f32[2,2,32,128]{3,2,1,0:T(8,128)S(1)}, u32[]{:S(2)}, u32[]{:S(2)}) %collective-permute-start.10) | collective-permute-done | bytes 65568 | tf_op jit(solution)/shard_map/ppermute | solution.py:468
  60.0 2.9 %shard_map.91 = f32[2,16,256,256]{3,2,1,0:T(8,128)} custom-call(s32[16]{0:T(128)S(1)} %copy-done.5, f32[2,16,384,128]{3,2,1,0:T(8,128)S(1)} %get-tuple-element.19.far, f32[2,16,384,128]{3,2,1,0:T(8,128)S(1)} %get-tuple-element.21.own, f32[2,2,384,128]{3,2,1,0:T(8,128)S(1)} %get-tuple-element.30.g, ...), custom_call_target="tpu_custom_call", output_to_operand_aliasing={{}: (6, {})} | custom-call | tf_op jit(solution)/shard_map/pallas_call | solution.py:447
  (22 shorter events, 0.5 us)
Async XLA Ops:
  2.4 7.0 %copy-start = (f32[2,256,256]{2,1,0:T(8,128)S(1)}, f32[2,256,256]{2,1,0:T(8,128)}, u32[]{:S(2)}) copy-start(f32[2,256,256]{2,1,0:T(8,128)} %probe.5) | copy-start | bytes 1572868
  2.4 7.0 %copy-start.2 = (f32[8,256,256]{2,1,0:T(8,128)S(1)}, f32[8,256,256]{2,1,0:T(8,128)}, u32[]{:S(2)}) copy-start(f32[8,256,256]{2,1,0:T(8,128)} %amps.1) | copy-start | bytes 6291460
  2.4 7.0 %copy-start.4 = (bf16[256,256]{1,0:T(8,128)(2,1)S(1)}, bf16[256,256]{1,0:T(8,128)(2,1)}, u32[]{:S(2)}) copy-start(bf16[256,256]{1,0:T(8,128)(2,1)} %constant.8.clone.pick) | copy-start | bytes 393220
  2.4 10.8 %collective-permute-start.2 = (f32[320,128]{1,0:T(8,128)S(1)}, f32[320,128]{1,0:T(8,128)S(1)}, u32[]{:S(2)}, u32[]{:S(2)}) collective-permute-start(f32[320,128]{1,0:T(8,128)S(1)} %get-tuple-element.24), channel_id=1, source_target_pairs={{0,3},{1,2},{2,1},{3,0},{4,7},{5,6},{6,5},{7,4},{8,11},{9,10},{10,... | collective-permute-start | bytes 491528 | tf_op jit(solution)/shard_map/ppermute | solution.py:463
  6.2 26.9 %copy-start.1 = (bf16[8,128,384]{2,1,0:T(8,128)(2,1)S(1)}, bf16[8,128,384]{2,1,0:T(8,128)(2,1)}, u32[]{:S(2)}) copy-start(bf16[8,128,384]{2,1,0:T(8,128)(2,1)} %constant.6.clone.lefts) | copy-start | bytes 2359300
  6.2 26.9 %copy-start.6 = (s32[8]{0:T(128)S(1)}, s32[8]{0:T(128)}, u32[]{:S(2)}) copy-start(s32[8]{0:T(128)} %starts.3) | copy-start | bytes 100
  6.3 7.0 %collective-permute-start.1 = (f32[320,128]{1,0:T(8,128)S(1)}, f32[320,128]{1,0:T(8,128)S(1)}, u32[]{:S(2)}, u32[]{:S(2)}) collective-permute-start(f32[320,128]{1,0:T(8,128)S(1)} %get-tuple-element.20.rest_0_), channel_id=1, source_target_pairs={{0,2},{1,3},{2,0},{3,1},{4,6},{5,7},{6,4},{7,5},{8,10},{9,11},{10,... | collective-permute-start | bytes 491528 | tf_op jit(solution)/shard_map/ppermute | solution.py:463
  8.7 30.7 %copy-start.3 = (bf16[4,768,256]{2,1,0:T(8,128)(2,1)S(1)}, bf16[4,768,256]{2,1,0:T(8,128)(2,1)}, u32[]{:S(2)}) copy-start(bf16[4,768,256]{2,1,0:T(8,128)(2,1)} %constant.7.clone.rights) | copy-start | bytes 4718596
  8.7 5.3 %collective-permute-start = (f32[320,128]{1,0:T(8,128)S(1)}, f32[320,128]{1,0:T(8,128)S(1)}, u32[]{:S(2)}, u32[]{:S(2)}) collective-permute-start(f32[320,128]{1,0:T(8,128)S(1)} %get-tuple-element.23), channel_id=1, source_target_pairs={{0,1},{1,0},{2,3},{3,2},{4,5},{5,4},{6,7},{7,6},{8,9},{9,8},{10,11... | collective-permute-start | bytes 491528 | tf_op jit(solution)/shard_map/ppermute | solution.py:463
  14.1 41.4 %copy-start.5 = (s32[16]{0:T(128)S(1)}, s32[16]{0:T(128)}, u32[]{:S(2)}) copy-start(s32[16]{0:T(128)} %shears.3) | copy-start | bytes 196
  14.1 5.8 %collective-permute-start.3 = (f32[320,128]{1,0:T(8,128)S(1)}, f32[320,128]{1,0:T(8,128)S(1)}, u32[]{:S(2)}, u32[]{:S(2)}) collective-permute-start(f32[320,128]{1,0:T(8,128)S(1)} %shard_map.85.own), channel_id=1, source_target_pairs={{0,4},{1,5},{2,6},{3,7},{4,0},{5,1},{6,2},{7,3},{8,12},{9,13},{10,... | collective-permute-start | bytes 491528 | tf_op jit(solution)/shard_map/ppermute | solution.py:463
  19.8 8.7 %collective-permute-start.5 = (f32[160,128]{1,0:T(8,128)S(1)}, f32[160,128]{1,0:T(8,128)S(1)}, u32[]{:S(2)}, u32[]{:S(2)}) collective-permute-start(f32[160,128]{1,0:T(8,128)S(1)} %get-tuple-element.28), channel_id=1, source_target_pairs={{8,0},{16,8},{24,16},{32,24},{40,32},{48,40},{56,48},{64,56},{72,6... | collective-permute-start | bytes 245768 | tf_op jit(solution)/shard_map/ppermute | solution.py:468
  24.5 4.0 %collective-permute-start.4 = (f32[32,128]{1,0:T(8,128)S(1)}, f32[32,128]{1,0:T(8,128)S(1)}, u32[]{:S(2)}, u32[]{:S(2)}) collective-permute-start(f32[32,128]{1,0:T(8,128)S(1)} %get-tuple-element.27), channel_id=1, source_target_pairs={{0,8},{8,16},{16,24},{24,32},{32,40},{40,48},{48,56},{56,64},{64,7... | collective-permute-start | bytes 49160 | tf_op jit(solution)/shard_map/ppermute | solution.py:468
  28.5 4.6 %collective-permute-start.6 = (f32[384,128]{1,0:T(8,128)S(1)}, f32[384,128]{1,0:T(8,128)S(1)}, u32[]{:S(2)}, u32[]{:S(2)}) collective-permute-start(f32[384,128]{1,0:T(8,128)S(1)} %shard_map.87.own), channel_id=1, source_target_pairs={{0,1},{1,0},{2,3},{3,2},{4,5},{5,4},{6,7},{7,6},{8,9},{9,8},{10,11... | collective-permute-start | bytes 589832 | tf_op jit(solution)/shard_map/ppermute | solution.py:463
  29.4 6.1 %collective-permute-start.8 = (f32[384,128]{1,0:T(8,128)S(1)}, f32[384,128]{1,0:T(8,128)S(1)}, u32[]{:S(2)}, u32[]{:S(2)}) collective-permute-start(f32[384,128]{1,0:T(8,128)S(1)} %shard_map.87.own), channel_id=1, source_target_pairs={{0,3},{1,2},{2,1},{3,0},{4,7},{5,6},{6,5},{7,4},{8,11},{9,10},{10,... | collective-permute-start | bytes 589832 | tf_op jit(solution)/shard_map/ppermute | solution.py:463
  31.6 7.8 %collective-permute-start.7 = (f32[384,128]{1,0:T(8,128)S(1)}, f32[384,128]{1,0:T(8,128)S(1)}, u32[]{:S(2)}, u32[]{:S(2)}) collective-permute-start(f32[384,128]{1,0:T(8,128)S(1)} %shard_map.87.own), channel_id=1, source_target_pairs={{0,2},{1,3},{2,0},{3,1},{4,6},{5,7},{6,4},{7,5},{8,10},{9,11},{10,... | collective-permute-start | bytes 589832 | tf_op jit(solution)/shard_map/ppermute | solution.py:463
  47.6 12.4 %collective-permute-start.9 = (f32[2,2,160,128]{3,2,1,0:T(8,128)S(1)}, f32[2,2,160,128]{3,2,1,0:T(8,128)S(1)}, u32[]{:S(2)}, u32[]{:S(2)}) collective-permute-start(f32[2,2,160,128]{3,2,1,0:T(8,128)S(1)} %get-tuple-element.31), channel_id=1, source_target_pairs={{0,8},{8,16},{16,24},{24,32},{32,40},{40,48},{48,56},{56,64},{64,7... | collective-permute-start | bytes 983048 | tf_op jit(solution)/shard_map/ppermute | solution.py:468
  53.5 6.5 %collective-permute-start.10 = (f32[2,2,32,128]{3,2,1,0:T(8,128)S(1)}, f32[2,2,32,128]{3,2,1,0:T(8,128)S(1)}, u32[]{:S(2)}, u32[]{:S(2)}) collective-permute-start(f32[2,2,32,128]{3,2,1,0:T(8,128)S(1)} %get-tuple-element.32), channel_id=1, source_target_pairs={{8,0},{16,8},{24,16},{32,24},{40,32},{48,40},{56,48},{64,56},{72,6... | collective-permute-start | bytes 196616 | tf_op jit(solution)/shard_map/ppermute | solution.py:468
